TPU v7x, 128 devices: a whole 4x4x4 slice. The times are simulated.
128 devices in a mesh: ctx: 16 (over y, z_lo, core), kv: 8 (over x, z_hi).
Axes of the slice: x: 4, y: 4, z: 4 (z_hi: 2, z_lo: 2; z = z_hi * 2 + z_lo), core: 2. Of those that a mesh axis runs over, the one named last changes fastest.
Arguments:
- prompt_in: bfloat16 [256, 8192], P(None, 'ctx'), may hold values from -6 to 6
- step_in: bfloat16 [3, 64, 8192], P(None, None, 'ctx'), may hold values from -6 to 6
- norm_gain: bfloat16 [8192], P('ctx'), may hold values from 0.099609375 to 1.8984375
- query_weight: bfloat16 [8192, 8192], P('ctx', 'kv'), may hold values from -0.125 to 0.125
- key_weight: bfloat16 [8192, 1024], P('ctx', 'kv'), may hold values from -0.125 to 0.125
- value_weight: bfloat16 [8192, 1024], P('ctx', 'kv'), may hold values from -0.0625 to 0.0625
- out_weight: bfloat16 [8192, 8192], P('kv', 'ctx'), may hold values from -0.125 to 0.125
- key_cache: bfloat16 [8, 131072, 128], P('kv', 'ctx'), may hold values from -540 to 540
- value_cache: bfloat16 [8, 131072, 128], P('kv', 'ctx'), may hold values from -5 to 5
- cache_lengths: int32 [16], P('ctx'), may hold values from 2048 to 8192
- visible: int32 [64], replicated, may hold values from 1 to 256, as said below
Outputs:
- prompt_out: bfloat16 [256, 8192], P('kv', 'ctx')
- step_out: bfloat16 [3, 64, 8192], P(None, 'kv', 'ctx')
Inputs may be any that keep to these rules, and one draw needn't show every extreme that they name: `visible`: prompt tokens seen by each decode row.
All inputs are finite; a program needn't handle non-finite values.
Results may differ from a plain program's by a relative error of at most 0.035.
Values may be sent and summed in bfloat16 or wider, within the bound.
A program may use at most 192 MiB of HBM per device.

v0:
```python
import jax
import jax.numpy as jnp
from jax import lax
from jax.sharding import PartitionSpec as P

D = 8192
HD = 128
EPSILON = 1e-05


def normalize_rows(inputs, norm_gain):
    widened = inputs.astype(jnp.float32)
    scaled = (widened * norm_gain.astype(jnp.float32)).astype(jnp.bfloat16)
    squares = jnp.sum(widened * widened, axis=-1)
    return (scaled, squares)


def shard_attention(queries, key_shard, value_shard, length, extra_pairs, extra_mask):
    flat_rows, head_size = queries.shape
    block_rows = 512
    blocks = flat_rows // block_rows
    extra_count = extra_pairs.shape[0]
    slots_live = lax.broadcasted_iota(jnp.int32, (1, key_shard.shape[0]), 1) < length
    extra_keys = extra_pairs[:, :head_size]
    extra_values = extra_pairs[:, head_size:]
    factor = head_size ** (-0.5)

    def one_block(operands):
        query_block, mask_block = operands
        cache_scores = (
            jnp.einsum("fd,cd->fc", query_block, key_shard, preferred_element_type=jnp.float32)
            * factor
        )
        extra_scores = (
            jnp.einsum("fd,ed->fe", query_block, extra_keys, preferred_element_type=jnp.float32)
            * factor
        )
        cache_scores = jnp.where(slots_live, cache_scores, -jnp.inf)
        extra_scores = jnp.where(mask_block, extra_scores, -jnp.inf)
        highest = jnp.maximum(jnp.max(cache_scores, axis=1), jnp.max(extra_scores, axis=1))
        cache_weights = jnp.exp(cache_scores - highest[:, None]).astype(jnp.bfloat16)
        extra_weights = jnp.exp(extra_scores - highest[:, None]).astype(jnp.bfloat16)
        totals = jnp.sum(cache_weights, axis=1, dtype=jnp.float32) + jnp.sum(
            extra_weights, axis=1, dtype=jnp.float32
        )
        mixture = jnp.dot(cache_weights, value_shard, preferred_element_type=jnp.float32)
        mixture = mixture + jnp.dot(extra_weights, extra_values, preferred_element_type=jnp.float32)
        return (highest, totals, mixture)

    highest, totals, mixture = lax.map(
        one_block,
        (
            queries.reshape(blocks, block_rows, head_size),
            extra_mask.reshape(blocks, block_rows, extra_count),
        ),
    )
    return (
        highest.reshape(flat_rows),
        totals.reshape(flat_rows),
        mixture.reshape(flat_rows, head_size),
    )


def run_section(
    inputs,
    limits,
    owner_rows,
    owner_steps,
    store_fn,
    stores,
    norm_gain,
    query_weight,
    pair_weight,
    out_weight,
    key_shard,
    value_shard,
    length,
):
    step_sets, row_count, _ = inputs.shape
    device_place = lax.axis_index("ctx")
    owned_rows = row_count // lax.axis_size("ctx")
    scaled, squares = normalize_rows(inputs, norm_gain)
    query_part = jnp.einsum("srd,de->sre", scaled, query_weight, preferred_element_type=jnp.float32)
    pair_part = jnp.einsum("srd,de->rse", scaled, pair_weight, preferred_element_type=jnp.float32)
    query_sum, square_sum = lax.psum((query_part, squares), "ctx")
    pair_sum = lax.psum_scatter(
        pair_part.astype(jnp.bfloat16), "ctx", scatter_dimension=0, tiled=True
    ).astype(jnp.float32)
    inverse = lax.rsqrt(square_sum / D + EPSILON)
    queries = (query_sum * inverse[:, :, None]).astype(jnp.bfloat16)
    own_inverse = jnp.swapaxes(
        lax.dynamic_slice_in_dim(inverse, device_place * owned_rows, owned_rows, 1), 0, 1
    )
    pair_rows = (pair_sum * own_inverse[:, :, None]).astype(jnp.bfloat16)
    prompt_pairs, own_pairs = store_fn(pair_rows, stores)
    extra_pairs = jnp.concatenate(
        [prompt_pairs, own_pairs.reshape(-1, own_pairs.shape[-1])], axis=0
    )
    prompt_own = prompt_pairs.shape[0]
    rows_own = own_pairs.shape[0]
    step_total = own_pairs.shape[1]
    prompt_index = device_place * prompt_own + lax.broadcasted_iota(
        jnp.int32, (1, 1, prompt_own), 2
    )
    seen_prompt = prompt_index < limits[:, :, None]
    slot_ids = lax.broadcasted_iota(jnp.int32, (1, 1, rows_own * step_total), 2)
    slot_row = device_place * rows_own + slot_ids // step_total
    slot_step = slot_ids % step_total
    seen_own = (slot_row == owner_rows[:, :, None]) & (slot_step <= owner_steps[:, :, None])
    seen_keys = jnp.concatenate([seen_prompt, seen_own], axis=2)
    heads_per = queries.shape[2] // HD
    extra_count = seen_keys.shape[2]
    extra_mask = jnp.broadcast_to(
        seen_keys[:, :, None, :], (step_sets, row_count, heads_per, extra_count)
    )
    extra_mask = extra_mask.reshape(step_sets * row_count * heads_per, extra_count)
    flat_queries = queries.reshape(step_sets * row_count * heads_per, HD)
    highest, totals, mixture = shard_attention(
        flat_queries, key_shard, value_shard, length, extra_pairs, extra_mask
    )
    overall = lax.pmax(highest, "ctx")
    rescale = jnp.exp(highest - overall)
    totals, mixture = (
        lax.psum((totals * rescale).astype(jnp.bfloat16), "ctx").astype(jnp.float32),
        lax.psum((mixture * rescale[:, None]).astype(jnp.bfloat16), "ctx").astype(jnp.float32),
    )
    attended = (mixture / totals[:, None]).astype(jnp.bfloat16)
    attended = attended.reshape(step_sets, row_count, heads_per * HD)
    my_share = lax.psum_scatter(
        jnp.einsum("srk,kd->rsd", attended, out_weight, preferred_element_type=jnp.float32).astype(
            jnp.bfloat16
        ),
        "kv",
        scatter_dimension=0,
        tiled=True,
    ).astype(jnp.float32)
    return (jnp.swapaxes(my_share, 0, 1).astype(jnp.bfloat16), (prompt_pairs, own_pairs))


def on_device(
    prompt_in,
    step_in,
    norm_gain,
    query_weight,
    key_weight,
    value_weight,
    out_weight,
    key_cache,
    value_cache,
    cache_lengths,
    visible,
):
    ctx_count = lax.axis_size("ctx")
    prompt_total = prompt_in.shape[0]
    row_total = visible.shape[0]
    step_total = step_in.shape[0]
    prompt_own = prompt_total // ctx_count
    rows_own = row_total // ctx_count
    pair_weight = jnp.concatenate([key_weight, value_weight], axis=1)
    pair_width = pair_weight.shape[1]
    shared = (
        norm_gain,
        query_weight,
        pair_weight,
        out_weight,
        key_cache[0],
        value_cache[0],
        cache_lengths[0],
    )
    stores = (
        jnp.zeros((prompt_own, pair_width), jnp.bfloat16),
        jnp.zeros((rows_own, step_total, pair_width), jnp.bfloat16),
    )

    def keep_prompt(pair_rows, current):
        return (pair_rows[:, 0, :], current[1])

    prompt_limits = lax.broadcasted_iota(jnp.int32, (1, prompt_total), 1) + 1
    nobody = jnp.full((1, prompt_total), -1, jnp.int32)
    prompt_out, stores = run_section(
        prompt_in[None], prompt_limits, nobody, nobody, keep_prompt, stores, *shared
    )
    row_ids = lax.broadcasted_iota(jnp.int32, (1, row_total), 1)
    outputs = []
    for step_index in range(step_total):

        def keep_one(pair_rows, current, step_index=step_index):
            return (
                current[0],
                lax.dynamic_update_slice_in_dim(current[1], pair_rows, step_index, 1),
            )

        step_ids = jnp.full((1, row_total), step_index, jnp.int32)
        result, stores = run_section(
            step_in[step_index : step_index + 1],
            visible[None, :],
            row_ids,
            step_ids,
            keep_one,
            stores,
            *shared
        )
        outputs.append(result)
    step_out = jnp.concatenate(outputs, axis=0)
    return (prompt_out[0], step_out)


def solution(mesh):
    placed = (
        P(None, "ctx"),
        P(None, None, "ctx"),
        P("ctx"),
        P("ctx", "kv"),
        P("ctx", "kv"),
        P("ctx", "kv"),
        P("kv", "ctx"),
        P("kv", "ctx", None),
        P("kv", "ctx", None),
        P("ctx"),
        P(),
    )
    return jax.shard_map(
        on_device,
        mesh=mesh,
        in_specs=placed,
        out_specs=(P("kv", "ctx"), P(None, "kv", "ctx")),
        check_vma=False,
    )
```

profile of v0, /device:TPU:0, one launch (start us, length us, event | category | flops | bytes accessed | tf_op | source)
XLA Modules:
  0.0 1040.7 jit_solution(12494352496434197446)
XLA Ops:
  9.9 1.6 fusion.30
  11.5 1.6 fusion.31
  13.1 1.6 fusion.32
  14.8 1.2 fusion.23
  17.0 2.4 convolution_bitcast_fusion
  19.4 1.9 convolution_bitcast_fusion.1
  21.3 1.8 convolution_bitcast_fusion.3
  23.1 1.9 convolution_bitcast_fusion.2
  25.0 1.1 fusion.35
  26.1 1.1 fusion.41
  27.3 31.0 %all-reduce.6 = (f32[1,256]{1,0:T(1,128)S(1)}, f32[1,64]{1,0:T(1,128)S(1)}, f32[1,64]{1,0:T(1,128)S(1)}, f32[1,64]{1,0:T(1,128)S(1)}) all-reduce(f32[1,256]{1,0:T(1,128)S(1)} %bitcast.209, f32[1,64]{1,0:T(1,128)S(1)} %bitcast.213, f32[1,64]{1,0:T(1,128)S(1)} %bitcast.212, ...), channel_id=1, replica_groups=mesh['ctx'=16,'kv'=8] {'ctx'}, use_global_device_ids=true, to_apply=%region_2.0 | all-reduce | flops 448 | bytes 3584 | tf_op jit(solution)/shard_map/psum | solution.py:85
  61.2 1.2 dynamic-slice
  63.9 63.7 %all-reduce.21.cloned.1.call-done = (bf16[64,1,256]{2,0,1:T(8,128)(2,1)}, bf16[64,1,256]{2,0,1:T(8,128)(2,1)}, bf16[64,1,256]{2,0,1:T(8,128)(2,1)}) async-done(((bf16[64,1,256]{2,0,1:T(8,128)(2,1)}, bf16[64,1,256]{2,0,1:T(8,128)(2,1)}, bf16[64,1,256]{2,0,1:T(8,128)(2,1)}), (bf16[64,1,256]{2,0,1:T(8,128)(2,1)}, bf16[64,1,256]{2,0,1:T(8,128)(2,1)}, ...) | async-done | bytes 98320
  129.9 115.8 %all-reduce.17.cloned.1.call-done = bf16[256,1,256]{2,1,0:T(2,128)(2,1)} async-done(((bf16[256,1,256]{2,1,0:T(2,128)(2,1)}), bf16[256,1,256]{2,1,0:T(2,128)(2,1)}) %all-reduce.17.cloned.1.call-update) | async-done | bytes 131088
  246.5 126.1 %all-reduce.19.cloned.1.call-done = (f32[1,256,1024]{2,1,0:T(8,128)}, f32[1,64,1024]{2,1,0:T(8,128)}, f32[1,64,1024]{2,1,0:T(8,128)}, f32[1,64,1024]{2,1,0:T(8,128)}) async-done(((f32[1,256,1024]{2,1,0:T(8,128)}, f32[1,64,1024]{2,1,0:T(8,128)}, f32[1,64,1024]{2,1,0:T(8,128)}, f32[1,64,1024]{2,1,0:T(8,128)}), (f32[1,256,1024]{2,1,0:T(8,128)}, f32[1,64,1024]{2,1,0:T(8,128)}, f32[1,64,1024]{2,1,0:T(8,128)}, ...) | async-done | bytes 1835024 | tf_op jit(solution)/shard_map/psum | solution.py:85
  372.6 1.3 multiply_convert_fusion
  374.2 110.1 %while.3 = (s32[]{:T(128)}, f32[4,512]{1,0:T(4,128)S(1)}, f32[4,512]{1,0:T(4,128)S(1)}, f32[4,512,128]{2,1,0:T(8,128)}, bf16[4,512,128]{2,1,0:T(8,128)(2,1)S(1)}...) while((s32[]{:T(128)}, f32[4,512]{1,0:T(4,128)S(1)}, ...), condition=%wide.region_9.10_spmd.clone, body=%wide.region_4.9_spmd.clone.sunk | while | flops 2192774144 | bytes 64227508 | solution.py:50
  375.0 8.6 fusion.144
  383.9 11.2 %convert_reduce_fusion.10 = (f32[512]{0:T(512)S(1)}, bf16[512,8192]{1,0:T(8,128)(2,1)}) fusion(f32[512]{0:T(512)S(1)} %max.55, f32[512,8192]{1,0:T(8,128)} %get-tuple-element.411, pred[8192]{0:T(1024)(128)(4,1)S(1)} %compare_reduce_fusion.2), kind=kLoop, calls=%fused_computation.1.clone.1 | loop fusion | flops 25165312 | bytes 25178112 | tf_op jit(solution)/shard_map/while/body/eval_jaxpr/reduce_sum | solution.py:43
  395.1 5.7 fusion.146
  402.5 8.6 fusion.144
  411.4 11.2 %convert_reduce_fusion.10 = (f32[512]{0:T(512)S(1)}, bf16[512,8192]{1,0:T(8,128)(2,1)}) fusion(f32[512]{0:T(512)S(1)} %max.55, f32[512,8192]{1,0:T(8,128)} %get-tuple-element.411, pred[8192]{0:T(1024)(128)(4,1)S(1)} %compare_reduce_fusion.2), kind=kLoop, calls=%fused_computation.1.clone.1 | loop fusion | flops 25165312 | bytes 25178112 | tf_op jit(solution)/shard_map/while/body/eval_jaxpr/reduce_sum | solution.py:43
  422.6 5.7 fusion.146
  430.0 8.6 fusion.144
  438.9 11.2 %convert_reduce_fusion.10 = (f32[512]{0:T(512)S(1)}, bf16[512,8192]{1,0:T(8,128)(2,1)}) fusion(f32[512]{0:T(512)S(1)} %max.55, f32[512,8192]{1,0:T(8,128)} %get-tuple-element.411, pred[8192]{0:T(1024)(128)(4,1)S(1)} %compare_reduce_fusion.2), kind=kLoop, calls=%fused_computation.1.clone.1 | loop fusion | flops 25165312 | bytes 25178112 | tf_op jit(solution)/shard_map/while/body/eval_jaxpr/reduce_sum | solution.py:43
  450.2 5.7 fusion.146
  457.6 8.6 fusion.144
  466.4 11.2 %convert_reduce_fusion.10 = (f32[512]{0:T(512)S(1)}, bf16[512,8192]{1,0:T(8,128)(2,1)}) fusion(f32[512]{0:T(512)S(1)} %max.55, f32[512,8192]{1,0:T(8,128)} %get-tuple-element.411, pred[8192]{0:T(1024)(128)(4,1)S(1)} %compare_reduce_fusion.2), kind=kLoop, calls=%fused_computation.1.clone.1 | loop fusion | flops 25165312 | bytes 25178112 | tf_op jit(solution)/shard_map/while/body/eval_jaxpr/reduce_sum | solution.py:43
  477.7 5.7 fusion.146
  484.4 1.2 multiply_convert_fusion.1
  485.6 9.7 fusion.88
  495.4 8.1 fusion.86
  503.8 19.0 %fusion.13 = (f32[512]{0:T(512)S(1)}, f32[512]{0:T(512)S(1)}, f32[512]{0:T(512)S(1)}, f32[512,8192]{1,0:T(8,128)}) fusion(pred[8192]{0:T(1024)(128)(4,1)S(1)} %iota_compare_fusion.1, f32[512,8192]{1,0:T(8,128)} %fusion.88, f32[512,8192]{1,0:T(8,128)} %fusion.86, bf16[512,128]{1,0:T(8,128)(2,1)S(1)} %squeeze.45, bf16[1,8192,128]{2,1,0:T(8,128)(2,1)S(1)} %bitcast.197), kind=kOutput, calls=%fused_computation.29 | convolution fusion | flops 1111489024 | bytes 52574208 | tf_op jit(solution)/shard_map/while/body/eval_jaxpr/fd,cd->fc/dot_general | solution.py:31
  523.2 55.9 %all-reduce.8 = (f32[2048]{0:T(1024)S(1)}, f32[512]{0:T(512)S(1)}, f32[512]{0:T(512)S(1)}, f32[512]{0:T(512)S(1)}) all-reduce(f32[2048]{0:T(1024)S(1)} %bitcast.201, f32[512]{0:T(512)S(1)} %max.51, f32[512]{0:T(512)S(1)} %max.50, f32[512]{0:T(512)S(1)} %max.49), channel_id=1, replica_groups=mesh['ctx'=16,'kv'=8] {'ctx'}, use_global_device_ids=true, to_apply=%region_10.11 | all-reduce | flops 3584 | bytes 28672 | tf_op jit(solution)/shard_map/pmax | solution.py:121
  579.1 25.1 %convert_reduce_fusion.4 = (f32[512]{0:T(512)S(1)}, bf16[512,8192]{1,0:T(8,128)(2,1)S(1)}, f32[512]{0:T(512)S(1)}, bf16[512,8192]{1,0:T(8,128)(2,1)}, f32[512]{0:T(512)S(1)}, /*index=5*/bf16[512,8192]{1,0:T(8,128)(2,1)}) fusion(f32[512]{0:T(512)S(1)} %max.49, f32[512,8192]{1,0:T(8,128)} %get-tuple-element.321, pred[8192]{0:T(1024)(128)(4,1)S(1)} %iota_compare_fusion.1, ...), kind=kLoop, calls=%fused_computation.26 | loop fusion | flops 75495936 | bytes 75517952 | tf_op jit(solution)/shard_map/while/body/eval_jaxpr/reduce_sum | solution.py:43
  604.3 5.7 fusion.80
  610.0 5.8 fusion.82
  615.9 2.3 fusion.84
  618.3 2.4 fusion.33
  623.4 27.8 %all-reduce.9 = (bf16[2048]{0:T(1024)(128)(2,1)S(1)}, bf16[512]{0:T(512)(128)(2,1)S(1)}, bf16[512]{0:T(512)(128)(2,1)S(1)}, bf16[512]{0:T(512)(128)(2,1)S(1)}) all-reduce(bf16[2048]{0:T(1024)(128)(2,1)S(1)} %get-tuple-element.297, bf16[512]{0:T(512)(128)(2,1)S(1)} %get-tuple-element.293, ...), channel_id=1, replica_groups=mesh['ctx'=16,'kv'=8] {'ctx'}, use_global_device_ids=true, to_apply=%region_12.13 | all-reduce | flops 3584 | bytes 14336 | tf_op jit(solution)/shard_map/psum | solution.py:124
  651.3 90.8 %all-reduce.23.cloned.1.call-done = (bf16[2048,128]{1,0:T(8,128)(2,1)}, bf16[512,128]{1,0:T(8,128)(2,1)}, bf16[512,128]{1,0:T(8,128)(2,1)}, bf16[512,128]{1,0:T(8,128)(2,1)}) async-done(((bf16[2048,128]{1,0:T(8,128)(2,1)}, bf16[512,128]{1,0:T(8,128)(2,1)}, bf16[512,128]{1,0:T(8,128)(2,1)}, bf16[512,128]{1,0:T(8,128)(2,1)}), (bf16[2048,128]{1,0:T(8,128)(2,1)}, bf16[512,128]{1,0:T(8,128)(2,1)}, ...) | async-done | bytes 917520 | tf_op jit(solution)/shard_map/psum | solution.py:125
  742.0 1.4 divide_convert_fusion
  750.0 1.1 fusion.19
  751.1 65.1 %reduce-scatter.14.cloned.1.call-done = bf16[8,1,512]{2,0,1:T(8,128)(2,1)} async-done(((bf16[64,1,512]{2,0,1:T(8,128)(2,1)}), bf16[8,1,512]{2,0,1:T(8,128)(2,1)}) %reduce-scatter.14.cloned.1.call-update) | async-done | bytes 8208 | tf_op jit(solution)/shard_map/reduce_scatter | solution.py:129
  816.2 72.2 %reduce-scatter.12.cloned.1.call-done = bf16[8,1,512]{2,0,1:T(8,128)(2,1)} async-done(((bf16[64,1,512]{2,0,1:T(8,128)(2,1)}), bf16[8,1,512]{2,0,1:T(8,128)(2,1)}) %reduce-scatter.12.cloned.1.call-update) | async-done | bytes 8208 | tf_op jit(solution)/shard_map/reduce_scatter | solution.py:129
  888.4 72.3 %reduce-scatter.10.cloned.1.call-done = bf16[8,1,512]{2,0,1:T(8,128)(2,1)} async-done(((bf16[64,1,512]{2,0,1:T(8,128)(2,1)}), bf16[8,1,512]{2,0,1:T(8,128)(2,1)}) %reduce-scatter.10.cloned.1.call-update) | async-done | bytes 8208 | tf_op jit(solution)/shard_map/reduce_scatter | solution.py:129
  960.6 1.3 pad_maximum_fusion
  962.0 71.9 %reduce-scatter.8.cloned.1.call-done = bf16[32,1,512]{2,0,1:T(8,128)(2,1)} async-done(((bf16[256,1,512]{2,0,1:T(8,128)(2,1)}), bf16[32,1,512]{2,0,1:T(8,128)(2,1)}) %reduce-scatter.8.cloned.1.call-update) | async-done | bytes 32784 | tf_op jit(solution)/shard_map/reduce_scatter | solution.py:129
  (155 shorter events, 27.9 us)
Async XLA Ops:
  7.2 9.8 copy-start
  7.2 120.4 %all-reduce.21.cloned.1.call-start = ((), (), s32[]{:S(2)}) async-start(), calls=%async_computation.10 | async-start | bytes 196608
  14.7 231.0 %all-reduce.17.cloned.1.call-start = ((), (), s32[]{:S(2)}) async-start(), calls=%async_computation.8 | async-start | bytes 524288
  16.9 355.7 %all-reduce.19.cloned.1.call-start = ((), (), s32[]{:S(2)}) async-start(), calls=%async_computation.9 | async-start | bytes 3670016 | tf_op jit(solution)/shard_map/psum | solution.py:85
  25.0 717.0 %all-reduce.23.cloned.1.call-start = ((), (), s32[]{:S(2)}) async-start(), calls=%async_computation.11 | async-start | bytes 1835008 | tf_op jit(solution)/shard_map/psum | solution.py:125
  374.2 110.1 %copy-start.5 = (f32[1,64,1024]{2,1,0:T(8,128)S(1)}, f32[1,64,1024]{2,1,0:T(8,128)}, u32[]{:S(2)}) copy-start(f32[1,64,1024]{2,1,0:T(8,128)} %get-tuple-element.265) | copy-start | bytes 786436
  383.6 11.5 %copy-start.6 = (bf16[8192,128]{1,0:T(8,128)(2,1)S(1)}, bf16[8192,128]{1,0:T(8,128)(2,1)}, u32[]{:S(2)}) copy-start(bf16[8192,128]{1,0:T(8,128)(2,1)} %get-tuple-element.449) | copy-start | bytes 6291460 | tf_op jit(solution)/shard_map/while
  411.1 11.5 %copy-start.6 = (bf16[8192,128]{1,0:T(8,128)(2,1)S(1)}, bf16[8192,128]{1,0:T(8,128)(2,1)}, u32[]{:S(2)}) copy-start(bf16[8192,128]{1,0:T(8,128)(2,1)} %get-tuple-element.449) | copy-start | bytes 6291460 | tf_op jit(solution)/shard_map/while
  438.6 11.5 %copy-start.6 = (bf16[8192,128]{1,0:T(8,128)(2,1)S(1)}, bf16[8192,128]{1,0:T(8,128)(2,1)}, u32[]{:S(2)}) copy-start(bf16[8192,128]{1,0:T(8,128)(2,1)} %get-tuple-element.449) | copy-start | bytes 6291460 | tf_op jit(solution)/shard_map/while
  466.1 11.5 %copy-start.6 = (bf16[8192,128]{1,0:T(8,128)(2,1)S(1)}, bf16[8192,128]{1,0:T(8,128)(2,1)}, u32[]{:S(2)}) copy-start(bf16[8192,128]{1,0:T(8,128)(2,1)} %get-tuple-element.449) | copy-start | bytes 6291460 | tf_op jit(solution)/shard_map/while
  484.3 11.1 %copy-start.2 = (bf16[8192,128]{1,0:T(8,128)(2,1)S(1)}, bf16[8192,128]{1,0:T(8,128)(2,1)}, u32[]{:S(2)}) copy-start(bf16[8192,128]{1,0:T(8,128)(2,1)} %get-tuple-element.481) | copy-start | bytes 6291460
  485.6 17.8 %copy-start.4 = (f32[1,64,1024]{2,1,0:T(8,128)S(1)}, f32[1,64,1024]{2,1,0:T(8,128)}, u32[]{:S(2)}) copy-start(f32[1,64,1024]{2,1,0:T(8,128)} %get-tuple-element.266) | copy-start | bytes 786436
  579.1 25.1 %copy-start.7 = (bf16[8192,128]{1,0:T(8,128)(2,1)S(1)}, bf16[8192,128]{1,0:T(8,128)(2,1)}, u32[]{:S(2)}) copy-start(bf16[8192,128]{1,0:T(8,128)(2,1)} %get-tuple-element.524) | copy-start | bytes 6291460
  610.0 134.8 %copy-start.3 = (bf16[1024,512]{1,0:T(8,128)(2,1)S(1)}, bf16[1024,512]{1,0:T(8,128)(2,1)}, u32[]{:S(2)}) copy-start(bf16[1024,512]{1,0:T(8,128)(2,1)} %param.19) | copy-start | bytes 3145732
  610.0 423.9 %copy-start.1 = (bf16[512,1024]{1,0:T(8,128)(2,1)S(1)}, bf16[512,1024]{1,0:T(8,128)(2,1)}, u32[]{:S(2)}) copy-start(bf16[512,1024]{1,0:T(8,128)(2,1)} %param.16) | copy-start | bytes 3145732
  623.4 192.8 %reduce-scatter.14.cloned.1.call-start = ((), (), s32[]{:S(2)}) async-start(), calls=%async_computation.7 | async-start | bytes 73728 | tf_op jit(solution)/shard_map/reduce_scatter | solution.py:129
  745.7 142.7 %reduce-scatter.12.cloned.1.call-start = ((), (), s32[]{:S(2)}) async-start(), calls=%async_computation.6 | async-start | bytes 73728 | tf_op jit(solution)/shard_map/reduce_scatter | solution.py:129
  748.9 211.7 %reduce-scatter.10.cloned.1.call-start = ((), (), s32[]{:S(2)}) async-start(), calls=%async_computation.5 | async-start | bytes 73728 | tf_op jit(solution)/shard_map/reduce_scatter | solution.py:129
  749.9 283.9 %reduce-scatter.8.cloned.1.call-start = ((), (), s32[]{:S(2)}) async-start(), calls=%async_computation.4 | async-start | bytes 294912 | tf_op jit(solution)/shard_map/reduce_scatter | solution.py:129
Sparse Core Ops, SparseCore 0:
  14.9 112.6 all-reduce.20
  130.2 115.4 all-reduce.16
  248.5 124.1 all-reduce.18
  623.5 118.4 all-reduce.22
  745.8 70.3 reduce-scatter.13
  819.6 68.7 reduce-scatter.11
  891.9 68.6 reduce-scatter.9
  964.8 69.0 reduce-scatter.7
where the time goes:
time: 1040 us
  waiting for transfers between devices  678 us (65%)
  matrix products  133 us (13%)
  blocking collectives  115 us (11%)
  other arithmetic  90.4 us (9%)
  between operations  16.3 us (2%)
    reduce_scatter x4, waiting for transfers between devices, run_section(): lax.psum_scatter(jnp.einsum('srk,kd->rsd', attended, out_weight, preferre...  281 us
    unnamed x10, waiting for transfers between devices  180 us
    psum x1, waiting for transfers between devices, run_section(): query_sum, square_sum = lax.psum((query_part, squares), 'ctx')  126 us
    psum x1, waiting for transfers between devices, run_section(): lax.psum((mixture * rescale[:, None]).astype(jnp.bfloat16), 'ctx')  90.8 us
    dot_general x7, matrix products, one_block(): jnp.einsum('fd,cd->fc', query_block, key_shard, preferred_element_type=jn...  71.2 us
    reduce_sum x5, other arithmetic, one_block(): jnp.sum(cache_weights, axis=1, dtype=jnp.float32)  69.8 us
    pmax x1, blocking collectives, run_section(): overall = lax.pmax(highest, 'ctx')  55.9 us
    dot_general x7, matrix products, one_block(): jnp.dot(cache_weights, value_shard, preferred_element_type=jnp.float32)  36.7 us
  transfers between devices with their start and end apart: 8, of which 8 were waited for; matrix products, arithmetic and copies ran while one was open for 2% of the time, Pallas kernels for 0%

commit v1 on v0

--- a/solution.py
+++ b/solution.py
@@ -122,7 +122,9 @@
     rescale = jnp.exp(highest - overall)
     totals, mixture = (
         lax.psum((totals * rescale).astype(jnp.bfloat16), "ctx").astype(jnp.float32),
-        lax.psum((mixture * rescale[:, None]).astype(jnp.bfloat16), "ctx").astype(jnp.float32),
+        jnp.sum(
+            lax.all_gather((mixture * rescale[:, None]).astype(jnp.bfloat16), "ctx"), axis=0
+        ).astype(jnp.float32),
     )
     attended = (mixture / totals[:, None]).astype(jnp.bfloat16)
     attended = attended.reshape(step_sets, row_count, heads_per * HD)

time: 1040 us -> 1010 us (0.971)
  matrix products: 133 us -> 104 us
  blocking collectives: 115 us -> 141 us
  other arithmetic: 90.4 us -> 72.2 us
  waiting for transfers between devices: 678 us -> 665 us
    psum x1 -> x0, waiting for transfers between devices: 90.8 us -> none  [run_section(): lax.psum((mixture * rescale[:, None]).astype(jnp.bfloat16), 'ctx')]
    all_gather x0 -> x4, waiting for transfers between devices: none -> 75 us  [run_section(): lax.all_gather((mixture * rescale[:, None]).astype(jnp.bfloat16), 'ctx')]
    psum x1, blocking collectives: 27.8 us -> 54.2 us  [run_section(): lax.psum((totals * rescale).astype(jnp.bfloat16), 'ctx').astype(jnp.float32)]
    dot_general x7, matrix products: 71.2 us -> 47.3 us  [one_block(): jnp.einsum('fd,cd->fc', query_block, key_shard, preferred_element_type=jn...]
    reduce_sum x5, other arithmetic: 69.8 us -> 46.2 us  [one_block(): jnp.sum(cache_weights, axis=1, dtype=jnp.float32)]
    dot_general x7, matrix products: 36.7 us -> 24.9 us  [one_block(): jnp.dot(cache_weights, value_shard, preferred_element_type=jnp.float32)]
    reduce_sum x0 -> x4, other arithmetic: none -> 10.5 us  [run_section(): jnp.sum(lax.all_gather((mixture * rescale[:, None]).astype(jnp.bfloat16),...]
    unnamed x10 -> x13, waiting for transfers between devices: 180 us -> 179 us
  transfers between devices with their start and end apart: 8 -> 11, of which waited for: 8 -> 9; matrix products, arithmetic and copies ran while one was open for 2% -> 6% of each run, Pallas kernels for 0% -> 0%
where the time goes in v1:
time: 1010 us
  waiting for transfers between devices  665 us (66%)
  blocking collectives  141 us (14%)
  matrix products  104 us (10%)
  other arithmetic  72.2 us (7%)
  between operations  16.4 us (2%)
    reduce_scatter x4, waiting for transfers between devices, run_section(): lax.psum_scatter(jnp.einsum('srk,kd->rsd', attended, out_weight, preferre...  284 us
    unnamed x13, waiting for transfers between devices  179 us
    psum x1, waiting for transfers between devices, run_section(): query_sum, square_sum = lax.psum((query_part, squares), 'ctx')  126 us
    all_gather x4, waiting for transfers between devices, run_section(): lax.all_gather((mixture * rescale[:, None]).astype(jnp.bfloat16), 'ctx')  75 us
    pmax x1, blocking collectives, run_section(): overall = lax.pmax(highest, 'ctx')  56.1 us
    psum x1, blocking collectives, run_section(): lax.psum((totals * rescale).astype(jnp.bfloat16), 'ctx').astype(jnp.float32)  54.2 us
    dot_general x7, matrix products, one_block(): jnp.einsum('fd,cd->fc', query_block, key_shard, preferred_element_type=jn...  47.3 us
    reduce_sum x5, other arithmetic, one_block(): jnp.sum(cache_weights, axis=1, dtype=jnp.float32)  46.2 us
  transfers between devices with their start and end apart: 11, of which 9 were waited for; matrix products, arithmetic and copies ran while one was open for 6% of the time, Pallas kernels for 0%

profile of v1, /device:TPU:0, one launch (start us, length us, event | category | flops | bytes accessed | tf_op | source)
XLA Modules:
  0.0 1008.8 jit_solution(3724497780582293028)
XLA Ops:
  10.0 1.6 fusion.30
  11.7 1.6 fusion.31
  17.1 2.4 convolution_bitcast_fusion
  19.5 1.8 convolution_bitcast_fusion.1
  21.4 1.8 convolution_bitcast_fusion.2
  23.2 1.8 convolution_bitcast_fusion.3
  27.4 31.1 %all-reduce.6 = (f32[1,256]{1,0:T(1,128)S(1)}, f32[1,64]{1,0:T(1,128)S(1)}, f32[1,64]{1,0:T(1,128)S(1)}, f32[1,64]{1,0:T(1,128)S(1)}) all-reduce(f32[1,256]{1,0:T(1,128)S(1)} %bitcast.238, f32[1,64]{1,0:T(1,128)S(1)} %bitcast.242, f32[1,64]{1,0:T(1,128)S(1)} %bitcast.241, ...), channel_id=1, replica_groups=mesh['ctx'=16,'kv'=8] {'ctx'}, use_global_device_ids=true, to_apply=%region_2.0 | all-reduce | flops 448 | bytes 3584 | tf_op jit(solution)/shard_map/psum | solution.py:85
  64.4 63.3 %all-reduce.19.cloned.1.call-done = (bf16[64,1,256]{2,0,1:T(8,128)(2,1)}, bf16[64,1,256]{2,0,1:T(8,128)(2,1)}, bf16[64,1,256]{2,0,1:T(8,128)(2,1)}) async-done(((bf16[64,1,256]{2,0,1:T(8,128)(2,1)}, bf16[64,1,256]{2,0,1:T(8,128)(2,1)}, bf16[64,1,256]{2,0,1:T(8,128)(2,1)}), (bf16[64,1,256]{2,0,1:T(8,128)(2,1)}, bf16[64,1,256]{2,0,1:T(8,128)(2,1)}, ...) | async-done | bytes 98320
  130.0 115.8 %all-reduce.15.cloned.1.call-done = bf16[256,1,256]{2,1,0:T(2,128)(2,1)} async-done(((bf16[256,1,256]{2,1,0:T(2,128)(2,1)}), bf16[256,1,256]{2,1,0:T(2,128)(2,1)}) %all-reduce.15.cloned.1.call-update) | async-done | bytes 131088
  246.6 126.1 %all-reduce.17.cloned.1.call-done = (f32[1,256,1024]{2,1,0:T(8,128)}, f32[1,64,1024]{2,1,0:T(8,128)}, f32[1,64,1024]{2,1,0:T(8,128)}, f32[1,64,1024]{2,1,0:T(8,128)}) async-done(((f32[1,256,1024]{2,1,0:T(8,128)}, f32[1,64,1024]{2,1,0:T(8,128)}, f32[1,64,1024]{2,1,0:T(8,128)}, f32[1,64,1024]{2,1,0:T(8,128)}), (f32[1,256,1024]{2,1,0:T(8,128)}, f32[1,64,1024]{2,1,0:T(8,128)}, f32[1,64,1024]{2,1,0:T(8,128)}, ...) | async-done | bytes 1835024 | tf_op jit(solution)/shard_map/psum | solution.py:85
  373.9 9.7 fusion.94
  383.6 8.1 fusion.96
  391.9 2.2 multiply_convert_fusion
  395.5 18.9 %fusion.13 = (f32[512]{0:T(512)S(1)}, f32[512]{0:T(512)S(1)}, f32[512]{0:T(512)S(1)}, f32[512,8192]{1,0:T(8,128)}) fusion(pred[8192]{0:T(1024)(128)(4,1)S(1)} %iota_compare_fusion.1, f32[512,8192]{1,0:T(8,128)} %fusion.96, f32[512,8192]{1,0:T(8,128)} %fusion.94, bf16[512,128]{1,0:T(8,128)(2,1)S(1)} %squeeze.45, bf16[1,8192,128]{2,1,0:T(8,128)(2,1)S(1)} %copy-done.2), kind=kOutput, calls=%fused_computation.29 | convolution fusion | flops 1111489024 | bytes 52574208 | tf_op jit(solution)/shard_map/while/body/eval_jaxpr/fd,cd->fc/dot_general | solution.py:31
  414.7 25.3 %convert_reduce_fusion.4 = (f32[512]{0:T(512)S(1)}, bf16[512,8192]{1,0:T(8,128)(2,1)S(1)}, f32[512]{0:T(512)S(1)}, bf16[512,8192]{1,0:T(8,128)(2,1)}, f32[512]{0:T(512)S(1)}, /*index=5*/bf16[512,8192]{1,0:T(8,128)(2,1)}) fusion(f32[512]{0:T(512)S(1)} %max.49, f32[512,8192]{1,0:T(8,128)} %get-tuple-element.317, pred[8192]{0:T(1024)(128)(4,1)S(1)} %iota_compare_fusion.1, ...), kind=kLoop, calls=%fused_computation.26 | loop fusion | flops 75495936 | bytes 75517952 | tf_op jit(solution)/shard_map/while/body/eval_jaxpr/reduce_sum | solution.py:43
  440.1 3.0 fusion.92
  443.1 49.1 %while.3 = (s32[]{:T(128)}, f32[4,512]{1,0:T(4,128)S(1)}, f32[4,512]{1,0:T(4,128)S(1)}, f32[4,512,128]{2,1,0:T(8,128)}, bf16[4,512,128]{2,1,0:T(8,128)(2,1)S(1)}...) while((s32[]{:T(128)}, f32[4,512]{1,0:T(4,128)S(1)}, ...), condition=%wide.region_9.10_spmd.clone, body=%wide.region_4.9_spmd.clone.sunk | while | flops 2192774144 | bytes 64228008 | solution.py:50
  443.9 2.7 fusion.148
  446.7 5.2 convert_reduce_fusion.10
  452.0 2.3 fusion.150
  456.1 2.7 fusion.148
  459.0 5.2 convert_reduce_fusion.10
  464.2 2.3 fusion.150
  468.4 2.7 fusion.148
  471.3 5.2 convert_reduce_fusion.10
  476.5 2.3 fusion.150
  480.7 2.7 fusion.148
  483.6 5.2 convert_reduce_fusion.10
  488.8 2.3 fusion.150
  492.2 56.1 %all-reduce.8 = (f32[2048]{0:T(1024)S(1)}, f32[512]{0:T(512)S(1)}, f32[512]{0:T(512)S(1)}, f32[512]{0:T(512)S(1)}) all-reduce(f32[2048]{0:T(1024)S(1)} %bitcast.230, f32[512]{0:T(512)S(1)} %max.51, f32[512]{0:T(512)S(1)} %max.50, f32[512]{0:T(512)S(1)} %max.49), channel_id=1, replica_groups=mesh['ctx'=16,'kv'=8] {'ctx'}, use_global_device_ids=true, to_apply=%region_10.11 | all-reduce | flops 3584 | bytes 28672 | tf_op jit(solution)/shard_map/pmax | solution.py:121
  548.3 1.8 fusion.20
  550.3 6.3 fusion.90
  557.6 6.3 fusion.88
  566.6 54.2 %all-reduce.9 = (bf16[256,8]{1,0:T(8,128)(2,1)S(1)}, bf16[64,8]{1,0:T(8,128)(2,1)S(1)}, bf16[64,8]{1,0:T(8,128)(2,1)S(1)}, bf16[64,8]{1,0:T(8,128)(2,1)S(1)}) all-reduce(bf16[256,8]{1,0:T(8,128)(2,1)S(1)} %div.99, bf16[64,8]{1,0:T(8,128)(2,1)S(1)} %div.117, bf16[64,8]{1,0:T(8,128)(2,1)S(1)} %div.111, ...), channel_id=1, replica_groups=mesh['ctx'=16,'kv'=8] {'ctx'}, use_global_device_ids=true, to_apply=%region_12.13 | all-reduce | flops 3584 | bytes 14336 | tf_op jit(solution)/shard_map/psum | solution.py:124
  620.8 1.9 reduce_sum.175
  622.8 1.9 reduce_sum.180
  624.7 29.7 %all-gather.14.cloned.1.call-done = bf16[8192,128]{1,0:T(8,128)(2,1)} async-done(((bf16[512,128]{1,0:T(8,128)(2,1)}), bf16[8192,128]{1,0:T(8,128)(2,1)}) %all-gather.14.cloned.1.call-update) | async-done | bytes 2097168 | tf_op jit(solution)/shard_map/all_gather | solution.py:126
  654.4 1.9 reduce_sum.185
  656.5 2.1 fusion.24
  658.9 2.1 fusion.25
  661.2 2.1 fusion.26
  663.4 45.3 %all-gather.8.cloned.1.call-done = bf16[16,2048,128]{2,1,0:T(8,128)(2,1)} async-done(((bf16[1,2048,128]{2,1,0:T(8,128)(2,1)}), bf16[16,2048,128]{2,1,0:T(8,128)(2,1)}) %all-gather.8.cloned.1.call-update) | async-done | bytes 8388624 | tf_op jit(solution)/shard_map/all_gather | solution.py:126
  708.7 4.8 reduce_sum.172
  714.0 2.4 fusion.19
  716.4 66.8 %reduce-scatter.10.cloned.1.call-done = bf16[8,1,512]{2,0,1:T(8,128)(2,1)} async-done(((bf16[64,1,512]{2,0,1:T(8,128)(2,1)}), bf16[8,1,512]{2,0,1:T(8,128)(2,1)}) %reduce-scatter.10.cloned.1.call-update) | async-done | bytes 8208 | tf_op jit(solution)/shard_map/reduce_scatter | solution.py:131
  783.2 72.8 %reduce-scatter.12.cloned.1.call-done = bf16[8,1,512]{2,0,1:T(8,128)(2,1)} async-done(((bf16[64,1,512]{2,0,1:T(8,128)(2,1)}), bf16[8,1,512]{2,0,1:T(8,128)(2,1)}) %reduce-scatter.12.cloned.1.call-update) | async-done | bytes 8208 | tf_op jit(solution)/shard_map/reduce_scatter | solution.py:131
  856.0 72.6 %reduce-scatter.14.cloned.1.call-done = bf16[8,1,512]{2,0,1:T(8,128)(2,1)} async-done(((bf16[64,1,512]{2,0,1:T(8,128)(2,1)}), bf16[8,1,512]{2,0,1:T(8,128)(2,1)}) %reduce-scatter.14.cloned.1.call-update) | async-done | bytes 8208 | tf_op jit(solution)/shard_map/reduce_scatter | solution.py:131
  929.9 72.4 %reduce-scatter.8.cloned.1.call-done = bf16[32,1,512]{2,0,1:T(8,128)(2,1)} async-done(((bf16[256,1,512]{2,0,1:T(8,128)(2,1)}), bf16[32,1,512]{2,0,1:T(8,128)(2,1)}) %reduce-scatter.8.cloned.1.call-update) | async-done | bytes 32784 | tf_op jit(solution)/shard_map/reduce_scatter | solution.py:131
  (166 shorter events, 33.5 us)
Async XLA Ops:
  7.2 10.0 copy-start
  7.2 120.5 %all-reduce.19.cloned.1.call-start = ((), (), s32[]{:S(2)}) async-start(), calls=%async_computation.14 | async-start | bytes 196608
  8.9 374.7 %copy-start.2 = (bf16[1,8192,128]{2,1,0:T(8,128)(2,1)S(1)}, bf16[1,8192,128]{2,1,0:T(8,128)(2,1)}, u32[]{:S(2)}) copy-start(bf16[1,8192,128]{2,1,0:T(8,128)(2,1)} %param.20) | copy-start | bytes 6291460
  14.9 230.9 %all-reduce.15.cloned.1.call-start = ((), (), s32[]{:S(2)}) async-start(), calls=%async_computation.12 | async-start | bytes 524288
  17.1 355.6 %all-reduce.17.cloned.1.call-start = ((), (), s32[]{:S(2)}) async-start(), calls=%async_computation.13 | async-start | bytes 3670016 | tf_op jit(solution)/shard_map/psum | solution.py:85
  25.1 595.7 %all-gather.10.cloned.1.call-start = ((), (), s32[]{:S(2)}) async-start(), calls=%async_computation.9 | async-start | bytes 2228224 | tf_op jit(solution)/shard_map/all_gather | solution.py:126
  373.9 17.8 %copy-start.4 = (f32[1,64,1024]{2,1,0:T(8,128)S(1)}, f32[1,64,1024]{2,1,0:T(8,128)}, u32[]{:S(2)}) copy-start(f32[1,64,1024]{2,1,0:T(8,128)} %get-tuple-element.266) | copy-start | bytes 786436
  414.7 25.3 %copy-start.5 = (bf16[1,8192,128]{2,1,0:T(8,128)(2,1)S(1)}, bf16[1,8192,128]{2,1,0:T(8,128)(2,1)}, u32[]{:S(2)}) copy-start(bf16[1,8192,128]{2,1,0:T(8,128)(2,1)} %param.21) | copy-start | bytes 6291460
  446.5 5.4 copy-start.6
  458.8 5.4 copy-start.6
  471.1 5.4 copy-start.6
  483.4 5.4 copy-start.6
  492.2 72.7 %copy-start.3 = (f32[4,512,128]{2,1,0:T(8,128)S(1)}, f32[4,512,128]{2,1,0:T(8,128)}, u32[]{:S(2)}) copy-start(f32[4,512,128]{2,1,0:T(8,128)} %get-tuple-element.138) | copy-start | bytes 3145732
  550.2 72.6 %all-gather.12.cloned.1.call-start = ((), (), s32[]{:S(2)}) async-start(), calls=%async_computation.10 | async-start | bytes 2228224 | tf_op jit(solution)/shard_map/all_gather | solution.py:126
  557.5 96.9 %all-gather.14.cloned.1.call-start = ((), (), s32[]{:S(2)}) async-start(), calls=%async_computation.11 | async-start | bytes 2228224 | tf_op jit(solution)/shard_map/all_gather | solution.py:126
  564.8 437.4 %copy-start.1 = (bf16[512,1024]{1,0:T(8,128)(2,1)S(1)}, bf16[512,1024]{1,0:T(8,128)(2,1)}, u32[]{:S(2)}) copy-start(bf16[512,1024]{1,0:T(8,128)(2,1)} %param.16) | copy-start | bytes 3145732
  564.8 143.8 %all-gather.8.cloned.1.call-start = ((), (), s32[]{:S(2)}) async-start(), calls=%async_computation.4 | async-start | bytes 8912896 | tf_op jit(solution)/shard_map/all_gather | solution.py:126
  566.1 217.1 %reduce-scatter.10.cloned.1.call-start = ((), (), s32[]{:S(2)}) async-start(), calls=%async_computation.6 | async-start | bytes 73728 | tf_op jit(solution)/shard_map/reduce_scatter | solution.py:131
  658.7 197.3 %reduce-scatter.12.cloned.1.call-start = ((), (), s32[]{:S(2)}) async-start(), calls=%async_computation.7 | async-start | bytes 73728 | tf_op jit(solution)/shard_map/reduce_scatter | solution.py:131
  661.0 267.5 %reduce-scatter.14.cloned.1.call-start = ((), (), s32[]{:S(2)}) async-start(), calls=%async_computation.8 | async-start | bytes 73728 | tf_op jit(solution)/shard_map/reduce_scatter | solution.py:131
  663.3 338.9 %reduce-scatter.8.cloned.1.call-start = ((), (), s32[]{:S(2)}) async-start(), calls=%async_computation.5 | async-start | bytes 294912 | tf_op jit(solution)/shard_map/reduce_scatter | solution.py:131
Sparse Core Ops, SparseCore 0:
  15.0 112.5 all-reduce.18
  130.3 115.4 all-reduce.14
  248.5 124.0 all-reduce.16
  550.3 32.6 all-gather.9
  584.7 34.3 all-gather.11
  620.8 33.6 all-gather.13
  656.2 52.3 all-gather.7
  712.6 70.5 reduce-scatter.9
  787.2 68.7 reduce-scatter.11
  859.8 68.7 reduce-scatter.13
  933.1 69.0 reduce-scatter.7
